TPU v7x, 32 devices: a whole 2x2x4 slice. The times are simulated.
32 devices in a mesh: groups: 2 (over y), frame: 4 (over z), patch: 2 (over x), head: 2 (over core).
Axes of the slice: x: 2, y: 2, z: 4, core: 2. Of those that a mesh axis runs over, the one named last changes fastest.
Arguments:
- video: bfloat16 [16, 8, 1152], P(('groups', 'frame'), 'patch'), parts along dimension 0, may hold values from -1.5 to 1.5
- gain_time: float32 [1152], replicated, may hold values from 0.1 to 1.9
- qkv_time: bfloat16 [1152, 3, 1152], P('frame', None, 'head'), may hold values from -0.5343196 to 0.5343196
- out_time: bfloat16 [1152, 1152], P('frame', 'head'), may hold values from -0.1875 to 0.1875
- gain_space: float32 [1152], replicated, may hold values from 0.1 to 1.9
- qkv_space: bfloat16 [1152, 3, 1152], P('frame', None, 'head'), may hold values from -0.5343196 to 0.5343196
- out_space: bfloat16 [1152, 1152], P('frame', 'head'), may hold values from -0.1875 to 0.1875
Outputs:
- result: float32 [16, 8, 1152], P(('groups', 'frame', 'patch')), parts along dimension 0
There are 2 independent parts, one for each index of `groups`. A program takes and returns all parts, laid end to end along the dimension named above; an argument that names none is the same for every part. Nothing has to cross between parts.
All inputs are finite; a program needn't handle non-finite values.
Results may differ from a plain program's by a relative error of at most 0.04.
Values may be sent and summed in bfloat16 or wider, within the bound.
A program may use at most 64 MiB of HBM per device.

v0:
```python
import jax
import jax.numpy as jnp
from jax import lax
from jax.sharding import PartitionSpec as P

HEAD_WIDTH = 72


def layer_norm(tokens, gain):
    value_rows = tokens.astype(jnp.float32)
    center = jnp.mean(value_rows, axis=-1, keepdims=True)
    spread = jnp.mean((value_rows - center) ** 2, axis=-1, keepdims=True)
    return ((value_rows - center) * lax.rsqrt(spread + 1e-06) * gain).astype(jnp.bfloat16)


def project_qkv(normed, weight):
    columns = weight.shape[1] * weight.shape[2]
    total = jnp.dot(
        normed, weight.reshape(weight.shape[0], columns), preferred_element_type=jnp.float32
    )
    return total.astype(jnp.bfloat16)


def project_out(attended, weight):
    return lax.dot_general(
        attended, weight, (((1,), (1,)), ((), ())), preferred_element_type=jnp.float32
    )


def attend(qkv, over_first):
    query_rows, key_rows, value_rows = (qkv[:, :, 0], qkv[:, :, 1], qkv[:, :, 2])
    factor = 1.0 / jnp.sqrt(jnp.float32(HEAD_WIDTH))
    if over_first:
        score_matrix = (
            jnp.einsum("abhd,cbhd->bhac", query_rows, key_rows, preferred_element_type=jnp.float32)
            * factor
        )
        attention_weights = jax.nn.softmax(score_matrix, axis=-1).astype(jnp.bfloat16)
        attention_output = jnp.einsum(
            "bhac,cbhd->abhd", attention_weights, value_rows, preferred_element_type=jnp.float32
        )
    else:
        score_matrix = (
            jnp.einsum("abhd,achd->ahbc", query_rows, key_rows, preferred_element_type=jnp.float32)
            * factor
        )
        attention_weights = jax.nn.softmax(score_matrix, axis=-1).astype(jnp.bfloat16)
        attention_output = jnp.einsum(
            "ahbc,achd->abhd", attention_weights, value_rows, preferred_element_type=jnp.float32
        )
    return attention_output.astype(jnp.bfloat16)


def mix_partial(tokens, gain, qkv_weight, out_weight, over_first):
    rows_a, rows_b, width = tokens.shape
    flat = tokens.reshape(rows_a * rows_b, width)
    normed = layer_norm(flat, gain)
    qkv = project_qkv(normed, qkv_weight).reshape(rows_a, rows_b, 3, -1, HEAD_WIDTH)
    attended = attend(qkv, over_first).reshape(rows_a * rows_b, -1)
    partial_value = project_out(attended, out_weight)
    rounded = lax.optimization_barrier(partial_value.astype(jnp.bfloat16)).astype(jnp.float32)
    return (flat, rounded)


def on_device(video, gain_time, qkv_time, out_time, gain_space, qkv_space, out_space):
    frame_size = lax.axis_size("frame")
    patch_size = lax.axis_size("patch")
    device_count = frame_size * patch_size
    series = lax.all_to_all(video, "frame", split_axis=1, concat_axis=0, tiled=True)
    qkv_time, out_time, qkv_space, out_space = (
        lax.all_gather(qkv_time, "frame", axis=0, tiled=True),
        lax.all_gather(out_time, "frame", axis=0, tiled=True),
        lax.all_gather(qkv_space, "frame", axis=0, tiled=True),
        lax.all_gather(out_space, "frame", axis=0, tiled=True),
    )
    frame_count, series_count, width = series.shape
    set_count = frame_count // device_count
    flat, rounded = mix_partial(series, gain_time, qkv_time, out_time, True)
    summed = (
        lax.psum(rounded.astype(jnp.bfloat16), "head")
        .astype(jnp.float32)
        .reshape(device_count, set_count, series_count, width)
    )
    resident = flat.reshape(device_count, set_count, series_count, width)
    after_time = (resident.astype(jnp.float32) + summed).astype(jnp.bfloat16)
    arrived = lax.all_to_all(
        after_time, ("frame", "patch"), split_axis=0, concat_axis=2, tiled=True
    )
    whole_frames = arrived.reshape(set_count, device_count * series_count, width)
    whole_frames = whole_frames.reshape(set_count, frame_size, patch_size, series_count, width)
    whole_frames = jnp.transpose(whole_frames, (0, 2, 1, 3, 4)).reshape(
        set_count, device_count * series_count, width
    )
    flat_space, rounded_space = mix_partial(whole_frames, gain_space, qkv_space, out_space, False)
    summed_space = lax.psum(rounded_space.astype(jnp.bfloat16), "head").astype(jnp.float32)
    result = flat_space.astype(jnp.float32) + summed_space
    return result.reshape(whole_frames.shape)


def solution(mesh):
    placed = (
        P(("groups", "frame"), "patch", None),
        P(),
        P("frame", None, "head"),
        P("frame", "head"),
        P(),
        P("frame", None, "head"),
        P("frame", "head"),
    )
    return jax.shard_map(
        on_device,
        mesh=mesh,
        in_specs=placed,
        out_specs=P(("groups", "frame", "patch"), None, None),
        check_vma=False,
    )
```

profile of v0, /device:TPU:0, one launch (start us, length us, event | category | flops | bytes accessed | tf_op | source)
XLA Modules:
  0.0 265.1 jit_solution(1438901559891736711)
XLA Ops:
  6.5 0.0 all-gather.5.cloned.1.call-start
  6.5 0.7 all-gather.5.cloned.1.call-update
  7.3 0.0 all-gather.7.cloned.1.call-start
  7.3 0.7 all-gather.7.cloned.1.call-update
  8.0 0.0 all-gather.9.cloned.1.call-start
  8.1 0.7 all-gather.9.cloned.1.call-update
  8.7 0.7 copy.33
  9.5 11.7 %all_to_all.8 = bf16[2,4,1152]{2,0,1:T(2,128)(2,1)S(1)} all-to-all(bf16[2,4,1152]{2,0,1:T(2,128)(2,1)S(1)} %copy.33), channel_id=1, replica_groups=mesh['groups'=2,'frame'=4,'patch'=2,'head'=2] {'frame'}, dimensions={1} | all-to-all | bytes 36864 | tf_op jit(solution)/shard_map/all_to_all | solution.py:69
  21.2 0.1 fusion.8
  21.3 0.2 multiply_reduce_fusion.1
  21.5 0.8 multiply_convert_fusion.1
  22.4 73.8 %all-gather.5.cloned.1.call-done = bf16[1152,3,576]{2,0,1:T(8,128)(2,1)} async-done(((bf16[288,3,576]{2,0,1:T(8,128)(2,1)}), bf16[1152,3,576]{2,0,1:T(8,128)(2,1)}) %all-gather.5.cloned.1.call-update) | async-done | bytes 3981328 | tf_op jit(solution)/shard_map/all_gather | solution.py:71
  96.2 6.6 %copy.34 = bf16[1152,3,576]{0,2,1:T(8,128)(2,1)} copy(bf16[1152,3,576]{2,0,1:T(8,128)(2,1)} %all-gather.5.cloned.1.call-done) | data formatting | bytes 7962624 | tf_op jit(solution)/shard_map/all_gather | solution.py:71
  102.8 3.4 %convolution_convert_fusion.3 = bf16[8,1728]{1,0:T(8,128)(2,1)S(1)} fusion(bf16[8,1152]{1,0:T(8,128)(2,1)S(1)} %convert_element_type.113, bf16[1152,1728]{0,1:T(8,128)(2,1)} %bitcast.105), kind=kOutput, calls=%fused_computation.5 | convolution fusion | flops 31864320 | bytes 4027392 | tf_op jit(solution)/shard_map/dot_general | solution.py:18
  106.2 0.2 reshape.202
  106.4 0.2 fusion.19
  106.6 0.2 fusion.6
  106.8 0.1 reshape.206
  106.9 24.9 %all-gather.7.cloned.1.call-done = bf16[1152,576]{1,0:T(8,128)(2,1)} async-done(((bf16[288,576]{1,0:T(8,128)(2,1)}), bf16[1152,576]{1,0:T(8,128)(2,1)}) %all-gather.7.cloned.1.call-update) | async-done | bytes 1327120 | tf_op jit(solution)/shard_map/all_gather | solution.py:72
  131.8 1.9 convolution_convert_fusion.2
  133.7 3.4 %psum.14 = bf16[8,1152]{1,0:T(8,128)(2,1)S(1)} all-reduce(bf16[8,1152]{1,0:T(8,128)(2,1)S(1)} %convolution_convert_fusion.2), channel_id=1, replica_groups=mesh['groups'=2,'frame'=4,'patch'=2,'head'=2] {'head'}, use_global_device_ids=true, to_apply=%region_4.0 | all-reduce | flops 9216 | bytes 36864 | tf_op jit(solution)/shard_map/psum | solution.py:80
  137.1 0.5 broadcast.115
  137.6 0.7 reduce.12
  138.3 0.7 reshape.220
  139.0 3.5 %all-to-all-start.1 = ((bf16[8,2,576]{2,1,0:T(2,128)(2,1)}), bf16[8,2,576]{2,1,0:T(2,128)(2,1)S(1)}, u32[]{:S(2)}, u32[]{:S(2)}) async-start(bf16[8,2,576]{2,1,0:T(2,128)(2,1)} %reshape.220), calls=%async_computation.1 | async-start | bytes 40960 | tf_op jit(solution)/shard_map/all_to_all | solution.py:86
  142.5 0.0 all-gather.11.cloned.1.call-start
  142.6 0.5 all-gather.11.cloned.1.call-update
  143.1 0.0 copy-start
  143.1 74.2 %all-gather.9.cloned.1.call-done = bf16[1152,3,576]{2,0,1:T(8,128)(2,1)} async-done(((bf16[288,3,576]{2,0,1:T(8,128)(2,1)}), bf16[1152,3,576]{2,0,1:T(8,128)(2,1)}) %all-gather.9.cloned.1.call-update) | async-done | bytes 3981328 | tf_op jit(solution)/shard_map/all_gather | solution.py:73
  217.3 6.6 %copy.42 = bf16[1152,3,576]{0,2,1:T(8,128)(2,1)} copy(bf16[1152,3,576]{2,0,1:T(8,128)(2,1)} %all-gather.9.cloned.1.call-done) | data formatting | bytes 7962624 | tf_op jit(solution)/shard_map/all_gather | solution.py:73
  223.9 0.0 all-to-all-done.1
  223.9 0.1 reshape.221
  224.0 0.1 fusion.16
  224.2 0.2 multiply_reduce_fusion
  224.3 0.0 copy-done
  224.3 0.1 multiply_convert_fusion
  224.4 3.4 %convolution_convert_fusion.1 = bf16[8,1728]{1,0:T(8,128)(2,1)S(1)} fusion(bf16[8,1152]{1,0:T(8,128)(2,1)S(1)} %convert_element_type.129, bf16[1152,1728]{0,1:T(8,128)(2,1)} %bitcast.104), kind=kOutput, calls=%fused_computation.3 | convolution fusion | flops 31864320 | bytes 4027392 | tf_op jit(solution)/shard_map/dot_general | solution.py:18
  227.8 0.2 reshape.208
  228.0 0.2 fusion.20
  228.2 0.2 fusion.7
  228.4 0.1 reshape.212
  228.5 24.2 %all-gather.11.cloned.1.call-done = bf16[1152,576]{1,0:T(8,128)(2,1)} async-done(((bf16[288,576]{1,0:T(8,128)(2,1)}), bf16[1152,576]{1,0:T(8,128)(2,1)}) %all-gather.11.cloned.1.call-update) | async-done | bytes 1327120 | tf_op jit(solution)/shard_map/all_gather | solution.py:74
  252.6 1.9 convolution_convert_fusion
  254.5 3.4 %psum.15 = bf16[8,1152]{1,0:T(8,128)(2,1)S(1)} all-reduce(bf16[8,1152]{1,0:T(8,128)(2,1)S(1)} %convolution_convert_fusion), channel_id=1, replica_groups=mesh['groups'=2,'frame'=4,'patch'=2,'head'=2] {'head'}, use_global_device_ids=true, to_apply=%region_9.0 | all-reduce | flops 9216 | bytes 36864 | tf_op jit(solution)/shard_map/psum | solution.py:95
  257.9 0.6 add_bitcast_fusion
  (16 shorter events, 0.2 us)
Async XLA Ops:
  6.5 89.7 %all-gather.5.cloned.1.call-start = ((), (), s32[]{:S(2)}) async-start(), calls=%async_computation.2 | async-start | bytes 5529600 | tf_op jit(solution)/shard_map/all_gather | solution.py:71
  7.3 124.5 %all-gather.7.cloned.1.call-start = ((), (), s32[]{:S(2)}) async-start(), calls=%async_computation.3 | async-start | bytes 1843200 | tf_op jit(solution)/shard_map/all_gather | solution.py:72
  8.0 209.3 %all-gather.9.cloned.1.call-start = ((), (), s32[]{:S(2)}) async-start(), calls=%async_computation.4 | async-start | bytes 5529600 | tf_op jit(solution)/shard_map/all_gather | solution.py:73
  139.0 84.9 %all-to-all-start.1 = ((bf16[8,2,576]{2,1,0:T(2,128)(2,1)}), bf16[8,2,576]{2,1,0:T(2,128)(2,1)S(1)}, u32[]{:S(2)}, u32[]{:S(2)}) async-start(bf16[8,2,576]{2,1,0:T(2,128)(2,1)} %reshape.220), calls=%async_computation.1 | async-start | bytes 40960 | tf_op jit(solution)/shard_map/all_to_all | solution.py:86
  142.5 110.1 %all-gather.11.cloned.1.call-start = ((), (), s32[]{:S(2)}) async-start(), calls=%async_computation.5 | async-start | bytes 1843200 | tf_op jit(solution)/shard_map/all_gather | solution.py:74
  143.1 81.2 %copy-start = (f32[1152]{0:T(1024)S(1)}, f32[1152]{0:T(1024)}, u32[]{:S(2)}) copy-start(f32[1152]{0:T(1024)} %param.11) | copy-start | bytes 13828
Sparse Core Ops, SparseCore 0:
  8.9 87.2 all-gather.4
  97.8 33.9 all-gather.6
  133.4 83.8 all-gather.8
  218.7 33.8 all-gather.10
where the time goes:
time: 266 us; the launch traced here: 265 us
  waiting for transfers between devices  200 us (75%)
  blocking collectives  18.6 us (7%)
  local copies, waits for them, and re-layouts  15.8 us (6%)
  between operations  13.3 us (5%)
  matrix products  11.2 us (4%)
  starting transfers between devices  3.66 us (1%)
  other arithmetic  2.8 us (1%)
    all_gather x1, waiting for transfers between devices, on_device(): lax.all_gather(qkv_space, 'frame', axis=0, tiled=True)  74.2 us
    all_gather x1, waiting for transfers between devices, on_device(): lax.all_gather(qkv_time, 'frame', axis=0, tiled=True)  73.8 us
    all_gather x1, waiting for transfers between devices, on_device(): lax.all_gather(out_time, 'frame', axis=0, tiled=True)  24.9 us
    all_gather x1, waiting for transfers between devices, on_device(): lax.all_gather(out_space, 'frame', axis=0, tiled=True)  24.2 us
    all_to_all x1, blocking collectives, on_device(): lax.all_to_all(video, 'frame', split_axis=1, concat_axis=0, tiled=True)  11.7 us
    dot_general x2, matrix products, project_qkv(): jnp.dot(normed, weight.reshape(weight.shape[0], columns), preferred_eleme...  6.82 us
    all_gather x1, local copies, waits for them, and re-layouts, on_device(): lax.all_gather(qkv_time, 'frame', axis=0, tiled=True)  6.59 us
    all_gather x1, local copies, waits for them, and re-layouts, on_device(): lax.all_gather(qkv_space, 'frame', axis=0, tiled=True)  6.58 us
  transfers between devices with their start and end apart: 5, of which 4 were waited for; matrix products, arithmetic and copies ran while one was open for 10% of the time, Pallas kernels for 0%

commit v1 on v0

--- a/solution.py
+++ b/solution.py
@@ -1,6 +1,11 @@
+import functools
+
 import jax
 import jax.numpy as jnp
+import numpy as np
 from jax import lax
+from jax.experimental import pallas as pl
+from jax.experimental.pallas import tpu as pltpu
 from jax.sharding import PartitionSpec as P
 
 HEAD_WIDTH = 72
@@ -97,6 +102,310 @@
     return result.reshape(whole_frames.shape)
 
 
+MESH = pl.DeviceIdType.MESH
+BF16 = jnp.bfloat16
+F32 = jnp.float32
+
+
+class Plan:
+    def __init__(self, mesh_shape, video, qkv):
+        self.frame_n = mesh_shape["frame"]
+        self.patch_n = mesh_shape["patch"]
+        self.head_n = mesh_shape["head"]
+        self.frames, self.patches, self.width = video
+        self.depth = qkv[0]
+        self.cols = qkv[2]
+        self.heads = self.cols // HEAD_WIDTH
+        self.time_len = self.frames * self.frame_n
+        self.space_len = self.patches * self.patch_n
+        self.rows = self.time_len * self.patches
+        self.own_rows = self.frames * self.patches
+        self.series = self.patches // self.frame_n
+        self.sets = self.frames // self.patch_n
+        self.part_rows = self.rows // self.patch_n
+        self.dest_rows = self.rows // self.frame_n
+
+    def moves_less(self):
+        divides = (
+            self.patches % self.frame_n == 0
+            and self.frames % self.patch_n == 0
+            and self.dest_rows % 8 == 0
+        )
+        tokens = 2 * self.rows * (4 * self.cols + 2 * self.width)
+        weights = 2 * (self.frame_n - 1) * self.depth * 4 * self.cols
+        return divides and tokens < weights
+
+
+def row_moves(plan):
+    rows, frames, patches = plan.rows, plan.frames, plan.patches
+    sources = plan.patch_n * rows
+    both = plan.head_n * rows
+    matrix = np.zeros((3 + plan.patch_n, rows, max(sources, both)), np.float32)
+    for t in range(plan.time_len):
+        for b in range(patches):
+            matrix[0, b * plan.time_len + t, t * patches + b] = 1
+    for f in range(plan.frame_n):
+        for p in range(plan.patch_n):
+            for s in range(plan.sets):
+                for b in range(patches):
+                    at = (f * plan.sets + s) * patches + b
+                    row = p * plan.part_rows + at
+                    frame = (f * plan.patch_n + p) * plan.sets + s
+                    matrix[1, row, b * plan.time_len + frame] = 1
+                    placed = ((f * plan.sets + s) * plan.patch_n + p) * patches + b
+                    for h in range(plan.head_n):
+                        matrix[2, placed, h * rows + row] = 1
+                    for mine in range(plan.patch_n):
+                        local = mine * plan.sets + s
+                        source = ((p * plan.frame_n + f) * frames + local) * patches + b
+                        matrix[3 + mine, placed, source] = 1
+    return jnp.asarray(matrix, BF16)
+
+
+def dot(a, b):
+    return jnp.dot(a, b, preferred_element_type=F32)
+
+
+def dot_t(a, b):
+    return lax.dot_general(a, b, (((1,), (1,)), ((), ())), preferred_element_type=F32)
+
+
+def attend_rows(query, key, value, length, heads):
+    cols = query.shape[1]
+    lane = lax.broadcasted_iota(jnp.int32, (length, cols), 1)
+    masks = [(lane >= i * HEAD_WIDTH) & (lane < (i + 1) * HEAD_WIDTH) for i in range(heads)]
+    factor = 1.0 / HEAD_WIDTH**0.5
+    pieces = []
+    for start in range(0, query.shape[0], length):
+        q, k, v = (x[start : start + length] for x in (query, key, value))
+        spread = jnp.concatenate([jnp.where(m, q, 0.0) for m in masks], axis=0).astype(BF16)
+        score = dot_t(spread, k.astype(BF16)) * factor
+        score = jnp.exp(score - jnp.max(score, axis=-1, keepdims=True))
+        weight = (score / jnp.sum(score, axis=-1, keepdims=True)).astype(BF16)
+        mixed = dot(weight, v.astype(BF16))
+        total = jnp.zeros((length, cols), F32)
+        for i, m in enumerate(masks):
+            total = total + jnp.where(m, mixed[i * length : (i + 1) * length], 0.0)
+        pieces.append(total)
+    return jnp.concatenate(pieces, axis=0) if len(pieces) > 1 else pieces[0]
+
+
+def normed_slice(slots, own, gain, width):
+    center = sum(jnp.sum(s, axis=-1, keepdims=True) for s in slots) * (1.0 / width)
+    spread = sum(jnp.sum((s - center) ** 2, axis=-1, keepdims=True) for s in slots) * (1.0 / width)
+    return ((own - center) * lax.rsqrt(spread + 1e-06) * gain).astype(BF16)
+
+
+def block_kernel(
+    plan, video, gain_t, gain_s, moves, wq_t_hbm, wo_t_hbm, wq_s_hbm, wo_s_hbm, result,
+    wq_t, wo_t, wq_s, wo_s, staged, gains, vid, base, after, part_t, got_t, part_s, got_s,
+    att_t, att_s, proj, proj_all, last, last_all,
+    w_sem, vid_sem, got_t_sem, got_s_sem, att_t_sem, att_s_sem, proj_sem, last_sem,
+):
+    g, f, p, h = (lax.axis_index(a) for a in ("groups", "frame", "patch", "head"))
+    fn, pn, hn, depth = plan.frame_n, plan.patch_n, plan.head_n, plan.depth
+
+    def place(df, dp, dh):
+        return (g, lax.rem(f + df, fn), lax.rem(p + dp, pn), lax.rem(h + dh, hn))
+
+    loads = [
+        pltpu.make_async_copy(src, dst, w_sem.at[i])
+        for i, (src, dst) in enumerate(
+            ((wq_t_hbm, wq_t), (wo_t_hbm, wo_t), (wq_s_hbm, wq_s), (wo_s_hbm, wo_s))
+        )
+    ]
+    for load in loads:
+        load.start()
+
+    barrier = pltpu.get_barrier_semaphore()
+    offsets = [
+        (df, dp, dh) for df in range(fn) for dp in range(pn) for dh in range(hn) if df + dp + dh
+    ]
+    for offset in offsets:
+        pl.semaphore_signal(barrier, inc=1, device_id=place(*offset), device_id_type=MESH)
+
+    for i in range(plan.frames):
+        staged[i * plan.patches : (i + 1) * plan.patches] = video[i].astype(F32)
+    for j in range(fn):
+        lanes = slice(j * depth, (j + 1) * depth)
+        vid[p, f, j] = staged[:, lanes].astype(BF16)
+        gains[0, j] = gain_t[:, lanes]
+        gains[1, j] = gain_s[:, lanes]
+    pl.semaphore_wait(barrier, len(offsets))
+
+    sent = []
+
+    def push(src, dst, sems, number, target):
+        copy = pltpu.make_async_remote_copy(
+            src_ref=src, dst_ref=dst, send_sem=sems.at[0, number], recv_sem=sems.at[1, number],
+            device_id=target, device_id_type=MESH,
+        )
+        copy.start()
+        sent.append(copy)
+        return copy
+
+    near = [
+        push(vid.at[p, f], vid.at[p, f], vid_sem, df, place(df, 0, 0)) for df in range(1, fn)
+    ]
+    far = [
+        push(vid.at[p, f], vid.at[p, f], vid_sem, dp * fn + df, place(df, dp, 0))
+        for dp in range(1, pn)
+        for df in range(fn)
+    ]
+
+    def spread_attention(normed, wq, part, got, got_sem, att, att_sem, length):
+        for kind in range(3):
+            product = dot(normed, wq[kind])
+            for j in range(fn):
+                piece = product[j * plan.dest_rows : (j + 1) * plan.dest_rows]
+                part[j, kind] = piece.astype(BF16)
+        copies = [
+            push(part.at[lax.rem(f + df, fn)], got.at[df - 1], got_sem, df, place(df, 0, 0))
+            for df in range(1, fn)
+        ]
+        total = [part[f, kind].astype(F32) for kind in range(3)]
+        for df, copy in enumerate(copies):
+            copy.wait_recv()
+            total = [total[kind] + got[df, kind].astype(F32) for kind in range(3)]
+        total = [t.astype(BF16).astype(F32) for t in total]
+        att[f] = attend_rows(*total, length, plan.heads).astype(BF16)
+        copies = [
+            push(att.at[f], att.at[f], att_sem, df, place(df, 0, 0)) for df in range(1, fn)
+        ]
+        for copy in copies:
+            copy.wait_recv()
+        return jnp.concatenate([att[j].astype(F32) for j in range(fn)], axis=0).astype(BF16)
+
+    for copy in near:
+        copy.wait_recv()
+
+    def series_slot(j):
+        return jnp.concatenate([vid[p, s, j].astype(F32) for s in range(fn)], axis=0)
+
+    normed = normed_slice(
+        [series_slot(j) for j in range(fn)], series_slot(f), gains[0, f], plan.width
+    )
+    normed = dot(moves[0][:, : plan.rows], normed).astype(BF16)
+    loads[0].wait()
+    attended = spread_attention(
+        normed, wq_t, part_t, got_t, got_t_sem, att_t, att_t_sem, plan.time_len
+    )
+    loads[1].wait()
+    partial_value = dot_t(attended, wo_t[...]).astype(BF16)
+    partial_value = dot(moves[1][:, : plan.rows], partial_value).astype(BF16)
+    for q in range(pn):
+        proj[q] = partial_value[q * plan.part_rows : (q + 1) * plan.part_rows]
+    copies = []
+    for number, offset in enumerate(offsets):
+        target = place(*offset)
+        copies.append(push(proj.at[target[2]], proj_all.at[h, p, f], proj_sem, number, target))
+    proj_all[h, p, f] = proj[p]
+
+    for copy in far:
+        copy.wait_recv()
+    for j in range(fn):
+        stacked = jnp.concatenate(
+            [vid[q, s, j].astype(F32) for q in range(pn) for s in range(fn)], axis=0
+        )
+        base[j] = dot(moves[3 + p][:, : pn * plan.rows], stacked.astype(BF16))
+    for copy in copies:
+        copy.wait_recv()
+    slots = []
+    for j in range(fn):
+        stacked = jnp.concatenate(
+            [proj_all[k, q, j].astype(F32) for k in range(hn) for q in range(pn)], axis=0
+        )
+        added = base[j] + dot(moves[2][:, : hn * plan.rows], stacked.astype(BF16))
+        slot = added.astype(BF16).astype(F32)
+        for s in range(fn):
+            after[j, s] = slot[s * plan.dest_rows : (s + 1) * plan.dest_rows]
+        slots.append(slot)
+    own = jnp.concatenate([after[f, s] for s in range(fn)], axis=0)
+    normed = normed_slice(slots, own, gains[1, f], plan.width)
+    loads[2].wait()
+    attended = spread_attention(
+        normed, wq_s, part_s, got_s, got_s_sem, att_s, att_s_sem, plan.space_len
+    )
+    loads[3].wait()
+    partial_value = dot_t(attended, wo_s[...])
+    for j in range(fn):
+        last[j] = partial_value[j * plan.dest_rows : (j + 1) * plan.dest_rows].astype(BF16)
+    copies = []
+    for dh in range(hn):
+        for df in range(fn):
+            if df + dh:
+                target = place(df, 0, dh)
+                number = dh * fn + df
+                copies.append(push(last.at[target[1]], last_all.at[h, f], last_sem, number, target))
+    last_all[h, f] = last[f]
+    for copy in copies:
+        copy.wait_recv()
+    for j in range(fn):
+        total = after[j, f]
+        for k in range(hn):
+            total = total + last_all[k, j].astype(F32)
+        result[:, j * depth : (j + 1) * depth] = total
+    for copy in sent:
+        copy.wait_send()
+
+
+def move_tokens(plan, video, gain_time, qkv_time, out_time, gain_space, qkv_space, out_space):
+    fn, pn, hn, depth, cols = plan.frame_n, plan.patch_n, plan.head_n, plan.depth, plan.cols
+    own, dest, rows = plan.own_rows, plan.dest_rows, plan.rows
+    vmem = pl.BlockSpec(memory_space=pltpu.VMEM)
+    hbm = pl.BlockSpec(memory_space=pl.ANY)
+    everyone = fn * pn * hn
+    pairs = lambda count: pltpu.SemaphoreType.DMA((2, count))
+    result = pl.pallas_call(
+        functools.partial(block_kernel, plan),
+        out_shape=jax.ShapeDtypeStruct((plan.sets * plan.space_len, plan.width), F32),
+        in_specs=[vmem] * 4 + [hbm] * 4,
+        out_specs=vmem,
+        scratch_shapes=[
+            pltpu.VMEM((3, depth, cols), BF16),
+            pltpu.VMEM((depth, cols), BF16),
+            pltpu.VMEM((3, depth, cols), BF16),
+            pltpu.VMEM((depth, cols), BF16),
+            pltpu.VMEM((own, plan.width), F32),
+            pltpu.VMEM((2, fn, 1, depth), F32),
+            pltpu.VMEM((pn, fn, fn, own, depth), BF16),
+            pltpu.VMEM((fn, rows, depth), F32),
+            pltpu.VMEM((fn, fn, dest, depth), F32),
+            pltpu.VMEM((fn, 3, dest, cols), BF16),
+            pltpu.VMEM((max(fn - 1, 1), 3, dest, cols), BF16),
+            pltpu.VMEM((fn, 3, dest, cols), BF16),
+            pltpu.VMEM((max(fn - 1, 1), 3, dest, cols), BF16),
+            pltpu.VMEM((fn, dest, cols), BF16),
+            pltpu.VMEM((fn, dest, cols), BF16),
+            pltpu.VMEM((pn, plan.part_rows, depth), BF16),
+            pltpu.VMEM((hn, pn, fn, plan.part_rows, depth), BF16),
+            pltpu.VMEM((fn, dest, depth), BF16),
+            pltpu.VMEM((hn, fn, dest, depth), BF16),
+            pltpu.SemaphoreType.DMA((4,)),
+            pairs(pn * fn),
+            pairs(fn),
+            pairs(fn),
+            pairs(fn),
+            pairs(fn),
+            pairs(everyone),
+            pairs(hn * fn),
+        ],
+        compiler_params=pltpu.CompilerParams(
+            collective_id=0, has_side_effects=True, vmem_limit_bytes=48 * 1024 * 1024
+        ),
+    )(
+        video,
+        gain_time.reshape(1, -1),
+        gain_space.reshape(1, -1),
+        row_moves(plan),
+        jnp.transpose(qkv_time, (1, 0, 2)),
+        out_time,
+        jnp.transpose(qkv_space, (1, 0, 2)),
+        out_space,
+    )
+    return result.reshape(plan.sets, plan.space_len, plan.width)
+
+
 def solution(mesh):
     placed = (
         P(("groups", "frame"), "patch", None),
@@ -107,8 +416,15 @@
         P("frame", None, "head"),
         P("frame", "head"),
     )
+
+    def on_one(video, gain_time, qkv_time, *others):
+        plan = Plan(mesh.shape, video.shape, qkv_time.shape)
+        if plan.moves_less():
+            return move_tokens(plan, video, gain_time, qkv_time, *others)
+        return on_device(video, gain_time, qkv_time, *others)
+
     return jax.shard_map(
-        on_device,
+        on_one,
         mesh=mesh,
         in_specs=placed,
         out_specs=P(("groups", "frame", "patch"), None, None),

time: 266 us -> 48.6 us (0.18)
  waiting for transfers between devices: 200 us -> 0 us
  Pallas kernels: 0 us -> 40.2 us
  blocking collectives: 18.6 us -> 0 us
  between operations: 13.3 us -> 0.02 us
  matrix products: 11.2 us -> 0 us
  local copies, waits for them, and re-layouts: 15.8 us -> 7.98 us
  starting transfers between devices: 3.66 us -> 0 us
  other arithmetic: 2.8 us -> 0 us
    all_gather x4 -> x0, waiting for transfers between devices: 197 us -> none  [the longest x1 74.2 us: on_device(): lax.all_gather(qkv_space, 'frame', axis=0, tiled=True)]
    pallas_call x0 -> x1, Pallas kernels: none -> 40.2 us  [move_tokens(): pl.pallas_call(functools.partial(block_kernel, plan), out_shape=jax.Shape...]
    all_gather x2 -> x0, local copies, waits for them, and re-layouts: 13.2 us -> none  [the longest x1 6.59 us: on_device(): lax.all_gather(qkv_time, 'frame', axis=0, tiled=True)]
    all_to_all x1 -> x0, blocking collectives: 11.7 us -> none  [on_device(): lax.all_to_all(video, 'frame', split_axis=1, concat_axis=0, tiled=True)]
    dot_general x6 -> x0, matrix products: 10.9 us -> none  [the longest x2 6.82 us: project_qkv(): jnp.dot(normed, weight.reshape(weight.shape[0], columns), preferred_eleme...]
    psum x2 -> x0, blocking collectives: 6.85 us -> none  [the longest x1 3.43 us: on_device(): lax.psum(rounded.astype(jnp.bfloat16), 'head').astype(jnp.float32)]
    unnamed x5 -> x13, local copies, waits for them, and re-layouts: 1.55 us -> 6.58 us
    all_to_all x1 -> x0, starting transfers between devices: 3.55 us -> none  [on_device(): lax.all_to_all(after_time, ('frame', 'patch'), split_axis=0, concat_axis=...]
  transfers between devices with their start and end apart: 5 -> 0, of which waited for: 4 -> 0; matrix products, arithmetic and copies ran while one was open for 10% -> 0% of each run, Pallas kernels for 0% -> 0%
where the time goes in v1:
time: 48.6 us; the launch traced here: 48.2 us
  Pallas kernels  40.2 us (83%)
  local copies, waits for them, and re-layouts  7.98 us (16%)
    pallas_call x1, Pallas kernels, move_tokens(): pl.pallas_call(functools.partial(block_kernel, plan), out_shape=jax.Shape...  40.2 us
    unnamed x13, local copies, waits for them, and re-layouts  6.58 us

profile of v1, /device:TPU:0, one launch (start us, length us, event | category | flops | bytes accessed | tf_op | source)
XLA Modules:
  0.0 48.2 jit_solution(5256152658942162331)
XLA Ops:
  0.0 0.7 %reshape.9.gain_t = f32[1,1152]{1,0:T(1,128)S(1)} reshape(f32[1152]{0:T(1024)} %param.9) | data formatting | bytes 9216 | tf_op jit(solution)/shard_map/reshape | solution.py:398
  0.7 0.7 %reshape.10.gain_s = f32[1,1152]{1,0:T(1,128)S(1)} reshape(f32[1152]{0:T(1024)} %param.12) | data formatting | bytes 9216 | tf_op jit(solution)/shard_map/reshape | solution.py:399
  1.4 0.0 copy-start
  1.4 1.2 %copy-done = bf16[288,3,576]{2,0,1:T(8,128)(2,1)S(1)} copy-done((bf16[288,3,576]{2,0,1:T(8,128)(2,1)S(1)}, bf16[288,3,576]{2,0,1:T(8,128)(2,1)}, u32[]{:S(2)}) %copy-start) | copy-done | bytes 995352
  2.6 0.0 copy-start.1
  2.6 1.2 %copy-done.1 = bf16[288,3,576]{2,0,1:T(8,128)(2,1)S(1)} copy-done((bf16[288,3,576]{2,0,1:T(8,128)(2,1)S(1)}, bf16[288,3,576]{2,0,1:T(8,128)(2,1)}, u32[]{:S(2)}) %copy-start.1) | copy-done | bytes 995352
  3.9 0.0 copy-start.2
  3.9 1.0 %copy-done.2 = bf16[288,576]{1,0:T(8,128)(2,1)S(1)} copy-done((bf16[288,576]{1,0:T(8,128)(2,1)S(1)}, bf16[288,576]{1,0:T(8,128)(2,1)}, u32[]{:S(2)}) %copy-start.2) | copy-done | bytes 331800
  4.9 0.0 copy-start.3
  4.9 1.0 %copy-done.3 = bf16[288,576]{1,0:T(8,128)(2,1)S(1)} copy-done((bf16[288,576]{1,0:T(8,128)(2,1)S(1)}, bf16[288,576]{1,0:T(8,128)(2,1)}, u32[]{:S(2)}) %copy-start.3) | copy-done | bytes 331800
  5.9 0.0 copy-start.4
  5.9 0.8 %copy-done.4 = bf16[5,32,64]{2,1,0:T(8,128)(2,1)S(1)} copy-done((bf16[5,32,64]{2,1,0:T(8,128)(2,1)S(1)}, bf16[5,32,64]{2,1,0:T(8,128)(2,1)}, u32[]{:S(2)}) %copy-start.4) | copy-done | bytes 20504
  6.6 0.0 copy-start.5
  6.6 0.7 %copy-done.5 = bf16[2,4,1152]{2,1,0:T(4,128)(2,1)S(1)} copy-done((bf16[2,4,1152]{2,1,0:T(4,128)(2,1)S(1)}, bf16[2,4,1152]{2,1,0:T(4,128)(2,1)}, u32[]{:S(2)}) %copy-start.5) | copy-done | bytes 18456
  7.4 40.2 %shard_map.82 = f32[8,1152]{1,0:T(8,128)S(1)} custom-call(bf16[2,4,1152]{2,1,0:T(4,128)(2,1)S(1)} %copy-done.5, f32[1,1152]{1,0:T(1,128)S(1)} %reshape.9.gain_t, f32[1,1152]{1,0:T(1,128)S(1)} %reshape.10.gain_s, bf16[5,32,64]{2,1,0:T(8,128)(2,1)S(1)} %copy-done.4, bf16[3,288,576]{2,1,0:T(8,128)(2,1)S(1)} %bitcast.3, bf16[288,576]{1,0:T(8,128)(2,1)S(1)} %copy-done.2, ...), custom_call_target="tpu_custom_call" | custom-call | tf_op jit(solution)/shard_map/pallas_call | solution.py:359
  47.5 0.6 %copy.10 = f32[1,8,1152]{2,1,0:T(8,128)} copy(f32[1,8,1152]{2,1,0:T(8,128)S(1)} %bitcast.5) | data formatting | bytes 73728
Async XLA Ops:
  1.4 1.2 %copy-start = (bf16[288,3,576]{2,0,1:T(8,128)(2,1)S(1)}, bf16[288,3,576]{2,0,1:T(8,128)(2,1)}, u32[]{:S(2)}) copy-start(bf16[288,3,576]{2,0,1:T(8,128)(2,1)} %param.10) | copy-start | bytes 2985988
  2.6 1.2 %copy-start.1 = (bf16[288,3,576]{2,0,1:T(8,128)(2,1)S(1)}, bf16[288,3,576]{2,0,1:T(8,128)(2,1)}, u32[]{:S(2)}) copy-start(bf16[288,3,576]{2,0,1:T(8,128)(2,1)} %param.13) | copy-start | bytes 2985988
  3.9 1.0 %copy-start.2 = (bf16[288,576]{1,0:T(8,128)(2,1)S(1)}, bf16[288,576]{1,0:T(8,128)(2,1)}, u32[]{:S(2)}) copy-start(bf16[288,576]{1,0:T(8,128)(2,1)} %wo_t_hbm.1) | copy-start | bytes 995332
  4.9 1.0 %copy-start.3 = (bf16[288,576]{1,0:T(8,128)(2,1)S(1)}, bf16[288,576]{1,0:T(8,128)(2,1)}, u32[]{:S(2)}) copy-start(bf16[288,576]{1,0:T(8,128)(2,1)} %wo_s_hbm.1) | copy-start | bytes 995332
  5.9 0.8 %copy-start.4 = (bf16[5,32,64]{2,1,0:T(8,128)(2,1)S(1)}, bf16[5,32,64]{2,1,0:T(8,128)(2,1)}, u32[]{:S(2)}) copy-start(bf16[5,32,64]{2,1,0:T(8,128)(2,1)} %constant.2.clone.moves) | copy-start | bytes 61444
  6.6 0.7 %copy-start.5 = (bf16[2,4,1152]{2,1,0:T(4,128)(2,1)S(1)}, bf16[2,4,1152]{2,1,0:T(4,128)(2,1)}, u32[]{:S(2)}) copy-start(bf16[2,4,1152]{2,1,0:T(4,128)(2,1)} %video.1) | copy-start | bytes 55300

commit v2 on v1

--- a/solution.py
+++ b/solution.py
@@ -197,8 +197,8 @@
 
 
 def block_kernel(
-    plan, video, gain_t, gain_s, moves, wq_t_hbm, wo_t_hbm, wq_s_hbm, wo_s_hbm, result,
-    wq_t, wo_t, wq_s, wo_s, staged, gains, vid, base, after, part_t, got_t, part_s, got_s,
+    plan, video_hbm, gain_t_hbm, gain_s_hbm, moves_hbm, wq_t_hbm, wo_t_hbm, wq_s_hbm, wo_s_hbm,
+    result, video, gain_t, gain_s, moves, wq_t, wo_t, wq_s, wo_s, staged, gains, vid, base, after, part_t, got_t, part_s, got_s,
     att_t, att_s, proj, proj_all, last, last_all,
     w_sem, vid_sem, got_t_sem, got_s_sem, att_t_sem, att_s_sem, proj_sem, last_sem,
 ):
@@ -211,10 +211,13 @@
     loads = [
         pltpu.make_async_copy(src, dst, w_sem.at[i])
         for i, (src, dst) in enumerate(
-            ((wq_t_hbm, wq_t), (wo_t_hbm, wo_t), (wq_s_hbm, wq_s), (wo_s_hbm, wo_s))
+            (
+                (wq_t_hbm, wq_t), (wo_t_hbm, wo_t), (wq_s_hbm, wq_s), (wo_s_hbm, wo_s),
+                (video_hbm, video), (gain_t_hbm, gain_t), (gain_s_hbm, gain_s), (moves_hbm, moves),
+            )
         )
     ]
-    for load in loads:
+    for load in loads[4:] + loads[:4]:
         load.start()
 
     barrier = pltpu.get_barrier_semaphore()
@@ -224,13 +227,12 @@
     for offset in offsets:
         pl.semaphore_signal(barrier, inc=1, device_id=place(*offset), device_id_type=MESH)
 
+    loads[4].wait()
     for i in range(plan.frames):
         staged[i * plan.patches : (i + 1) * plan.patches] = video[i].astype(F32)
     for j in range(fn):
         lanes = slice(j * depth, (j + 1) * depth)
         vid[p, f, j] = staged[:, lanes].astype(BF16)
-        gains[0, j] = gain_t[:, lanes]
-        gains[1, j] = gain_s[:, lanes]
     pl.semaphore_wait(barrier, len(offsets))
 
     sent = []
@@ -252,6 +254,13 @@
         for dp in range(1, pn)
         for df in range(fn)
     ]
+
+    for load in loads[5:]:
+        load.wait()
+    for j in range(fn):
+        lanes = slice(j * depth, (j + 1) * depth)
+        gains[0, j] = gain_t[...].reshape(1, plan.width)[:, lanes]
+        gains[1, j] = gain_s[...].reshape(1, plan.width)[:, lanes]
 
     def spread_attention(normed, wq, part, got, got_sem, att, att_sem, length):
         for kind in range(3):
@@ -353,15 +362,20 @@
     fn, pn, hn, depth, cols = plan.frame_n, plan.patch_n, plan.head_n, plan.depth, plan.cols
     own, dest, rows = plan.own_rows, plan.dest_rows, plan.rows
     vmem = pl.BlockSpec(memory_space=pltpu.VMEM)
-    hbm = pl.BlockSpec(memory_space=pl.ANY)
+    hbm = pl.BlockSpec(memory_space=pltpu.HBM)
     everyone = fn * pn * hn
+    moves = row_moves(plan)
     pairs = lambda count: pltpu.SemaphoreType.DMA((2, count))
     result = pl.pallas_call(
         functools.partial(block_kernel, plan),
         out_shape=jax.ShapeDtypeStruct((plan.sets * plan.space_len, plan.width), F32),
-        in_specs=[vmem] * 4 + [hbm] * 4,
+        in_specs=[hbm] * 8,
         out_specs=vmem,
         scratch_shapes=[
+            pltpu.VMEM(video.shape, BF16),
+            pltpu.VMEM(gain_time.shape, F32),
+            pltpu.VMEM(gain_space.shape, F32),
+            pltpu.VMEM(moves.shape, BF16),
             pltpu.VMEM((3, depth, cols), BF16),
             pltpu.VMEM((depth, cols), BF16),
             pltpu.VMEM((3, depth, cols), BF16),
@@ -381,7 +395,7 @@
             pltpu.VMEM((hn, pn, fn, plan.part_rows, depth), BF16),
             pltpu.VMEM((fn, dest, depth), BF16),
             pltpu.VMEM((hn, fn, dest, depth), BF16),
-            pltpu.SemaphoreType.DMA((4,)),
+            pltpu.SemaphoreType.DMA((8,)),
             pairs(pn * fn),
             pairs(fn),
             pairs(fn),
@@ -391,13 +405,13 @@
             pairs(hn * fn),
         ],
         compiler_params=pltpu.CompilerParams(
-            collective_id=0, has_side_effects=True, vmem_limit_bytes=48 * 1024 * 1024
+            collective_id=0, has_side_effects=True, vmem_limit_bytes=63 * 1024 * 1024
         ),
     )(
         video,
-        gain_time.reshape(1, -1),
-        gain_space.reshape(1, -1),
-        row_moves(plan),
+        gain_time,
+        gain_space,
+        moves,
         jnp.transpose(qkv_time, (1, 0, 2)),
         out_time,
         jnp.transpose(qkv_space, (1, 0, 2)),

time: 48.6 us -> 41.6 us (0.86)
  local copies, waits for them, and re-layouts: 7.98 us -> 1.39 us
    unnamed x13 -> x1, local copies, waits for them, and re-layouts: 6.58 us -> 1.39 us
    reshape x2 -> x0, local copies, waits for them, and re-layouts: 1.4 us -> none  [the longest x1 0.7 us: move_tokens(): gain_time.reshape(1, -1)]
where the time goes in v2:
time: 41.6 us; the launch traced here: 41.4 us
  Pallas kernels  40 us (96%)
  local copies, waits for them, and re-layouts  1.39 us (3%)
    pallas_call x1, Pallas kernels, move_tokens(): pl.pallas_call(functools.partial(block_kernel, plan), out_shape=jax.Shape...  40 us
    unnamed x1, local copies, waits for them, and re-layouts  1.39 us

profile of v2, /device:TPU:0, one launch (start us, length us, event | category | flops | bytes accessed | tf_op | source)
XLA Modules:
  0.0 41.4 jit_solution(12969435961491218319)
XLA Ops:
  0.0 40.0 %shard_map.82 = f32[8,1152]{1,0:T(8,128)} custom-call(bf16[2,4,1152]{2,1,0:T(4,128)(2,1)} %video_hbm.1, f32[1152]{0:T(1024)} %gain_t_hbm.1, f32[1152]{0:T(1024)} %gain_s_hbm.1, bf16[5,32,64]{2,1,0:T(8,128)(2,1)} %constant.2.clone.moves_hbm, bf16[3,288,576]{2,1,0:T(8,128)(2,1)} %bitcast.3, bf16[288,576]{1,0:T(8,128)(2,1)} %wo_t_hbm.1, ...), custom_call_target="tpu_custom_call" | custom-call | tf_op jit(solution)/shard_map/pallas_call | solution.py:369
  40.0 1.4 %copy.10 = f32[1,8,1152]{2,1,0:T(8,128)} copy(f32[1,8,1152]{2,1,0:T(8,128)} %bitcast.5) | data formatting | bytes 73728

commit v3 on v2

--- a/solution.py
+++ b/solution.py
@@ -137,10 +137,8 @@
 
 
 def row_moves(plan):
-    rows, frames, patches = plan.rows, plan.frames, plan.patches
-    sources = plan.patch_n * rows
-    both = plan.head_n * rows
-    matrix = np.zeros((3 + plan.patch_n, rows, max(sources, both)), np.float32)
+    rows, patches = plan.rows, plan.patches
+    matrix = np.zeros((3, rows, rows), np.float32)
     for t in range(plan.time_len):
         for b in range(patches):
             matrix[0, b * plan.time_len + t, t * patches + b] = 1
@@ -153,12 +151,7 @@
                     frame = (f * plan.patch_n + p) * plan.sets + s
                     matrix[1, row, b * plan.time_len + frame] = 1
                     placed = ((f * plan.sets + s) * plan.patch_n + p) * patches + b
-                    for h in range(plan.head_n):
-                        matrix[2, placed, h * rows + row] = 1
-                    for mine in range(plan.patch_n):
-                        local = mine * plan.sets + s
-                        source = ((p * plan.frame_n + f) * frames + local) * patches + b
-                        matrix[3 + mine, placed, source] = 1
+                    matrix[2, placed, row] = 1
     return jnp.asarray(matrix, BF16)
 
 
@@ -199,8 +192,8 @@
 def block_kernel(
     plan, video_hbm, gain_t_hbm, gain_s_hbm, moves_hbm, wq_t_hbm, wo_t_hbm, wq_s_hbm, wo_s_hbm,
     result, video, gain_t, gain_s, moves, wq_t, wo_t, wq_s, wo_s, staged, gains, vid, base, after, part_t, got_t, part_s, got_s,
-    att_t, att_s, proj, proj_all, last, last_all,
-    w_sem, vid_sem, got_t_sem, got_s_sem, att_t_sem, att_s_sem, proj_sem, last_sem,
+    att_t, att_s, pair, proj, proj_all, last, last_all,
+    w_sem, vid_sem, got_t_sem, got_s_sem, att_t_sem, att_s_sem, pair_sem, proj_sem, last_sem,
 ):
     g, f, p, h = (lax.axis_index(a) for a in ("groups", "frame", "patch", "head"))
     fn, pn, hn, depth = plan.frame_n, plan.patch_n, plan.head_n, plan.depth
@@ -222,7 +215,11 @@
 
     barrier = pltpu.get_barrier_semaphore()
     offsets = [
-        (df, dp, dh) for df in range(fn) for dp in range(pn) for dh in range(hn) if df + dp + dh
+        (df, dp, dh)
+        for df in range(fn)
+        for dp in range(pn)
+        for dh in range(hn)
+        if df + dp + dh and (dp == 0 or dh == 0)
     ]
     for offset in offsets:
         pl.semaphore_signal(barrier, inc=1, device_id=place(*offset), device_id_type=MESH)
@@ -232,7 +229,7 @@
         staged[i * plan.patches : (i + 1) * plan.patches] = video[i].astype(F32)
     for j in range(fn):
         lanes = slice(j * depth, (j + 1) * depth)
-        vid[p, f, j] = staged[:, lanes].astype(BF16)
+        vid[f, j] = staged[:, lanes].astype(BF16)
     pl.semaphore_wait(barrier, len(offsets))
 
     sent = []
@@ -247,14 +244,8 @@
         return copy
 
     near = [
-        push(vid.at[p, f], vid.at[p, f], vid_sem, df, place(df, 0, 0)) for df in range(1, fn)
+        push(vid.at[f], vid.at[f], vid_sem, df, place(df, 0, 0)) for df in range(1, fn)
     ]
-    far = [
-        push(vid.at[p, f], vid.at[p, f], vid_sem, dp * fn + df, place(df, dp, 0))
-        for dp in range(1, pn)
-        for df in range(fn)
-    ]
-
     for load in loads[5:]:
         load.wait()
     for j in range(fn):
@@ -289,43 +280,47 @@
         copy.wait_recv()
 
     def series_slot(j):
-        return jnp.concatenate([vid[p, s, j].astype(F32) for s in range(fn)], axis=0)
+        return jnp.concatenate([vid[s, j].astype(F32) for s in range(fn)], axis=0)
 
     normed = normed_slice(
         [series_slot(j) for j in range(fn)], series_slot(f), gains[0, f], plan.width
     )
     normed = dot(moves[0][:, : plan.rows], normed).astype(BF16)
+    residual = dot(moves[0][:, : plan.rows], series_slot(f).astype(BF16)).astype(BF16)
+    base[...] = dot(moves[1][:, : plan.rows], residual)
     loads[0].wait()
     attended = spread_attention(
         normed, wq_t, part_t, got_t, got_t_sem, att_t, att_t_sem, plan.time_len
     )
     loads[1].wait()
     partial_value = dot_t(attended, wo_t[...]).astype(BF16)
-    partial_value = dot(moves[1][:, : plan.rows], partial_value).astype(BF16)
+    pair[0] = dot(moves[1][:, : plan.rows], partial_value).astype(BF16)
+    copies = [
+        push(pair.at[0], pair.at[dh], pair_sem, dh, place(0, 0, dh)) for dh in range(1, hn)
+    ]
+    total = pair[0].astype(F32)
+    for dh, copy in enumerate(copies):
+        copy.wait_recv()
+        total = total + pair[dh + 1].astype(F32)
+    total = (base[...] + total).astype(BF16)
     for q in range(pn):
-        proj[q] = partial_value[q * plan.part_rows : (q + 1) * plan.part_rows]
+        proj[q] = total[q * plan.part_rows : (q + 1) * plan.part_rows]
     copies = []
-    for number, offset in enumerate(offsets):
-        target = place(*offset)
-        copies.append(push(proj.at[target[2]], proj_all.at[h, p, f], proj_sem, number, target))
-    proj_all[h, p, f] = proj[p]
-
-    for copy in far:
-        copy.wait_recv()
-    for j in range(fn):
-        stacked = jnp.concatenate(
-            [vid[q, s, j].astype(F32) for q in range(pn) for s in range(fn)], axis=0
-        )
-        base[j] = dot(moves[3 + p][:, : pn * plan.rows], stacked.astype(BF16))
+    for dp in range(pn):
+        for df in range(fn):
+            if df + dp:
+                target = place(df, dp, 0)
+                number = dp * fn + df
+                copies.append(
+                    push(proj.at[target[2]], proj_all.at[p, f], proj_sem, number, target)
+                )
+    proj_all[p, f] = proj[p]
     for copy in copies:
         copy.wait_recv()
     slots = []
     for j in range(fn):
-        stacked = jnp.concatenate(
-            [proj_all[k, q, j].astype(F32) for k in range(hn) for q in range(pn)], axis=0
-        )
-        added = base[j] + dot(moves[2][:, : hn * plan.rows], stacked.astype(BF16))
-        slot = added.astype(BF16).astype(F32)
+        stacked = jnp.concatenate([proj_all[q, j].astype(F32) for q in range(pn)], axis=0)
+        slot = dot(moves[2][:, : plan.rows], stacked.astype(BF16))
         for s in range(fn):
             after[j, s] = slot[s * plan.dest_rows : (s + 1) * plan.dest_rows]
         slots.append(slot)
@@ -363,7 +358,6 @@
     own, dest, rows = plan.own_rows, plan.dest_rows, plan.rows
     vmem = pl.BlockSpec(memory_space=pltpu.VMEM)
     hbm = pl.BlockSpec(memory_space=pltpu.HBM)
-    everyone = fn * pn * hn
     moves = row_moves(plan)
     pairs = lambda count: pltpu.SemaphoreType.DMA((2, count))
     result = pl.pallas_call(
@@ -382,8 +376,8 @@
             pltpu.VMEM((depth, cols), BF16),
             pltpu.VMEM((own, plan.width), F32),
             pltpu.VMEM((2, fn, 1, depth), F32),
-            pltpu.VMEM((pn, fn, fn, own, depth), BF16),
-            pltpu.VMEM((fn, rows, depth), F32),
+            pltpu.VMEM((fn, fn, own, depth), BF16),
+            pltpu.VMEM((rows, depth), F32),
             pltpu.VMEM((fn, fn, dest, depth), F32),
             pltpu.VMEM((fn, 3, dest, cols), BF16),
             pltpu.VMEM((max(fn - 1, 1), 3, dest, cols), BF16),
@@ -391,17 +385,19 @@
             pltpu.VMEM((max(fn - 1, 1), 3, dest, cols), BF16),
             pltpu.VMEM((fn, dest, cols), BF16),
             pltpu.VMEM((fn, dest, cols), BF16),
+            pltpu.VMEM((hn, rows, depth), BF16),
             pltpu.VMEM((pn, plan.part_rows, depth), BF16),
-            pltpu.VMEM((hn, pn, fn, plan.part_rows, depth), BF16),
+            pltpu.VMEM((pn, fn, plan.part_rows, depth), BF16),
             pltpu.VMEM((fn, dest, depth), BF16),
             pltpu.VMEM((hn, fn, dest, depth), BF16),
             pltpu.SemaphoreType.DMA((8,)),
-            pairs(pn * fn),
             pairs(fn),
             pairs(fn),
             pairs(fn),
             pairs(fn),
-            pairs(everyone),
+            pairs(fn),
+            pairs(hn),
+            pairs(pn * fn),
             pairs(hn * fn),
         ],
         compiler_params=pltpu.CompilerParams(

time: 41.6 us -> 39.8 us (0.957)
  Pallas kernels: 40 us -> 38.2 us
    pallas_call x1, Pallas kernels: 40 us -> 38.2 us  [move_tokens(): pl.pallas_call(functools.partial(block_kernel, plan), out_shape=jax.Shape...]
where the time goes in v3:
time: 39.8 us; the launch traced here: 39.6 us
  Pallas kernels  38.2 us (96%)
  local copies, waits for them, and re-layouts  1.39 us (3%)
    pallas_call x1, Pallas kernels, move_tokens(): pl.pallas_call(functools.partial(block_kernel, plan), out_shape=jax.Shape...  38.2 us
    unnamed x1, local copies, waits for them, and re-layouts  1.39 us

profile of v3, /device:TPU:0, one launch (start us, length us, event | category | flops | bytes accessed | tf_op | source)
XLA Modules:
  0.0 39.6 jit_solution(14814690381957686415)
XLA Ops:
  0.0 38.2 %shard_map.82 = f32[8,1152]{1,0:T(8,128)} custom-call(bf16[2,4,1152]{2,1,0:T(4,128)(2,1)} %video_hbm.1, f32[1152]{0:T(1024)} %gain_t_hbm.1, f32[1152]{0:T(1024)} %gain_s_hbm.1, bf16[3,32,32]{2,1,0:T(8,128)(2,1)} %constant.2.clone.moves_hbm, bf16[3,288,576]{2,1,0:T(8,128)(2,1)} %bitcast.3, bf16[288,576]{1,0:T(8,128)(2,1)} %wo_t_hbm.1, ...), custom_call_target="tpu_custom_call" | custom-call | tf_op jit(solution)/shard_map/pallas_call | solution.py:363
  38.2 1.4 %copy.10 = f32[1,8,1152]{2,1,0:T(8,128)} copy(f32[1,8,1152]{2,1,0:T(8,128)} %bitcast.5) | data formatting | bytes 73728

commit v4 on v3

--- a/solution.py
+++ b/solution.py
@@ -191,7 +191,7 @@
 
 def block_kernel(
     plan, video_hbm, gain_t_hbm, gain_s_hbm, moves_hbm, wq_t_hbm, wo_t_hbm, wq_s_hbm, wo_s_hbm,
-    result, video, gain_t, gain_s, moves, wq_t, wo_t, wq_s, wo_s, staged, gains, vid, base, after, part_t, got_t, part_s, got_s,
+    result, video, gain_t, gain_s, moves, wq_t, wo_t, wq_s, wo_s, staged, gains, vid_out, vid, base, after, part_t, got_t, part_s, got_s,
     att_t, att_s, pair, proj, proj_all, last, last_all,
     w_sem, vid_sem, got_t_sem, got_s_sem, att_t_sem, att_s_sem, pair_sem, proj_sem, last_sem,
 ):
@@ -227,9 +227,16 @@
     loads[4].wait()
     for i in range(plan.frames):
         staged[i * plan.patches : (i + 1) * plan.patches] = video[i].astype(F32)
+    for load in loads[5:]:
+        load.wait()
+    tokens = staged[...]
+    gain = gain_t[...].reshape(1, plan.width)
+    normed = normed_slice([tokens], tokens, gain, plan.width).astype(F32)
     for j in range(fn):
         lanes = slice(j * depth, (j + 1) * depth)
-        vid[f, j] = staged[:, lanes].astype(BF16)
+        vid_out[j, 0] = staged[:, lanes].astype(BF16)
+        vid_out[j, 1] = normed[:, lanes].astype(BF16)
+        gains[0, j] = gain_s[...].reshape(1, plan.width)[:, lanes]
     pl.semaphore_wait(barrier, len(offsets))
 
     sent = []
@@ -243,15 +250,11 @@
         sent.append(copy)
         return copy
 
-    near = [
-        push(vid.at[f], vid.at[f], vid_sem, df, place(df, 0, 0)) for df in range(1, fn)
-    ]
-    for load in loads[5:]:
-        load.wait()
-    for j in range(fn):
-        lanes = slice(j * depth, (j + 1) * depth)
-        gains[0, j] = gain_t[...].reshape(1, plan.width)[:, lanes]
-        gains[1, j] = gain_s[...].reshape(1, plan.width)[:, lanes]
+    near = []
+    for df in range(1, fn):
+        target = place(df, 0, 0)
+        near.append(push(vid_out.at[target[1]], vid.at[f], vid_sem, df, target))
+    vid[f] = vid_out[f]
 
     def spread_attention(normed, wq, part, got, got_sem, att, att_sem, length):
         for kind in range(3):
@@ -279,14 +282,11 @@
     for copy in near:
         copy.wait_recv()
 
-    def series_slot(j):
-        return jnp.concatenate([vid[s, j].astype(F32) for s in range(fn)], axis=0)
-
-    normed = normed_slice(
-        [series_slot(j) for j in range(fn)], series_slot(f), gains[0, f], plan.width
-    )
-    normed = dot(moves[0][:, : plan.rows], normed).astype(BF16)
-    residual = dot(moves[0][:, : plan.rows], series_slot(f).astype(BF16)).astype(BF16)
+    def series(kind):
+        rows = jnp.concatenate([vid[s, kind].astype(F32) for s in range(fn)], axis=0).astype(BF16)
+        return dot(moves[0][:, : plan.rows], rows).astype(BF16)
+
+    normed, residual = series(1), series(0)
     base[...] = dot(moves[1][:, : plan.rows], residual)
     loads[0].wait()
     attended = spread_attention(
@@ -325,7 +325,7 @@
             after[j, s] = slot[s * plan.dest_rows : (s + 1) * plan.dest_rows]
         slots.append(slot)
     own = jnp.concatenate([after[f, s] for s in range(fn)], axis=0)
-    normed = normed_slice(slots, own, gains[1, f], plan.width)
+    normed = normed_slice(slots, own, gains[0, f], plan.width)
     loads[2].wait()
     attended = spread_attention(
         normed, wq_s, part_s, got_s, got_s_sem, att_s, att_s_sem, plan.space_len
@@ -375,8 +375,9 @@
             pltpu.VMEM((3, depth, cols), BF16),
             pltpu.VMEM((depth, cols), BF16),
             pltpu.VMEM((own, plan.width), F32),
-            pltpu.VMEM((2, fn, 1, depth), F32),
-            pltpu.VMEM((fn, fn, own, depth), BF16),
+            pltpu.VMEM((1, fn, 1, depth), F32),
+            pltpu.VMEM((fn, 2, own, depth), BF16),
+            pltpu.VMEM((fn, 2, own, depth), BF16),
             pltpu.VMEM((rows, depth), F32),
             pltpu.VMEM((fn, fn, dest, depth), F32),
             pltpu.VMEM((fn, 3, dest, cols), BF16),

time: 39.8 us -> 39.1 us (0.982)
  Pallas kernels: 38.2 us -> 37.5 us
    pallas_call x1, Pallas kernels: 38.2 us -> 37.5 us  [move_tokens(): pl.pallas_call(functools.partial(block_kernel, plan), out_shape=jax.Shape...]
where the time goes in v4:
time: 39.1 us; the launch traced here: 38.9 us
  Pallas kernels  37.5 us (96%)
  local copies, waits for them, and re-layouts  1.39 us (4%)
    pallas_call x1, Pallas kernels, move_tokens(): pl.pallas_call(functools.partial(block_kernel, plan), out_shape=jax.Shape...  37.5 us
    unnamed x1, local copies, waits for them, and re-layouts  1.39 us

profile of v4, /device:TPU:0, one launch (start us, length us, event | category | flops | bytes accessed | tf_op | source)
XLA Modules:
  0.0 38.9 jit_solution(4932922638497155425)
XLA Ops:
  0.0 37.5 %shard_map.82 = f32[8,1152]{1,0:T(8,128)} custom-call(bf16[2,4,1152]{2,1,0:T(4,128)(2,1)} %video_hbm.1, f32[1152]{0:T(1024)} %gain_t_hbm.1, f32[1152]{0:T(1024)} %gain_s_hbm.1, bf16[3,32,32]{2,1,0:T(8,128)(2,1)} %constant.2.clone.moves_hbm, bf16[3,288,576]{2,1,0:T(8,128)(2,1)} %bitcast.3, bf16[288,576]{1,0:T(8,128)(2,1)} %wo_t_hbm.1, ...), custom_call_target="tpu_custom_call" | custom-call | tf_op jit(solution)/shard_map/pallas_call | solution.py:363
  37.5 1.4 %copy.10 = f32[1,8,1152]{2,1,0:T(8,128)} copy(f32[1,8,1152]{2,1,0:T(8,128)} %bitcast.5) | data formatting | bytes 73728
